TPU v7x, 256 devices: a whole 4x4x8 slice. The times are simulated.
256 devices in a mesh: ctx: 64 (over x, z, core), lat: 4 (over y).
Axes of the slice: x: 4, y: 4, z: 8, core: 2. Of those that a mesh axis runs over, the one named last changes fastest.
Arguments:
- token_ids: int32 [32768], P('ctx'), may hold values from 0 to 255
- latent_offset: int32 [1], replicated, may hold values from 31616 to 31744
- embed_table: bfloat16 [256, 2048], replicated, may hold values from -6 to 6
- cross_q: bfloat16 [2048, 2048], P('ctx', 'lat')
- cross_kv: bfloat16 [2, 2048, 2048], P(None, 'ctx', 'lat')
- cross_out: bfloat16 [2048, 2048], P('lat'), may hold values from -0.375 to 0.375
- self_qkv: bfloat16 [3, 2048, 2048], P(None, None, 'lat')
- self_out: bfloat16 [2048, 2048], P('lat'), may hold values from -0.25 to 0.25
- mlp_in: bfloat16 [2048, 8192], P(None, 'ctx'), may hold values from -0.125 to 0.125
- mlp_out: bfloat16 [8192, 2048], P('ctx'), may hold values from -0.0625 to 0.0625
Outputs:
- latent_out: bfloat16 [4, 256, 2048], P('lat', 'ctx')
Inputs may be any that keep to these rules, and one draw needn't show every extreme that they name: `latent_offset`: the latent rows lie inside the context.
All inputs are finite; a program needn't handle non-finite values.
Results may differ from a plain program's by a relative error of at most 0.014.
Values may be sent and summed in bfloat16 or wider, within the bound.
A program may use at most 128 MiB of HBM per device.

v0:
```python
import math
import jax
import jax.numpy as jnp
from jax import lax
from jax.sharding import PartitionSpec as P

HD = 128
LATENTS = 1024
EPSILON = 1e-06
MASKED = -1e30


def sent_to_all(array, axis):
    count = lax.axis_size(axis)
    return lax.all_to_all(
        jnp.broadcast_to(array[None], (count, *array.shape)), axis, 0, 0, tiled=True
    )


def laid_out(pieces, dim):
    pieces = jnp.moveaxis(pieces, 0, dim)
    shape = pieces.shape
    return pieces.reshape(*shape[:dim], shape[dim] * shape[dim + 1], *shape[dim + 2 :])


def gathered_copies(array, axis, dim):
    pieces = sent_to_all(array, axis)
    return laid_out(pieces, dim)


def side_by_side(arrays, axis, split_dim, concat_dim, along):
    ends, at = ([], 0)
    for a in arrays[:-1]:
        at += a.shape[along]
        ends.append(at)
    both = jnp.concatenate(arrays, axis=along)
    return tuple(
        jnp.split(
            lax.all_to_all(both, axis, split_axis=split_dim, concat_axis=concat_dim, tiled=True),
            ends,
            axis=along,
        )
    )


def of_everyone(array, axis):
    return sent_to_all(array, axis).sum(axis=0)


def side_by_side_2(arrays, axis, dim, along):
    ends, at = ([], 0)
    for a in arrays[:-1]:
        at += a.shape[along]
        ends.append(at)
    both = jnp.concatenate(arrays, axis=along)
    return tuple(jnp.split(lax.all_gather(both, axis, axis=dim, tiled=True), ends, axis=along))


def over_copies(array, axis):
    everything = sent_to_all(array, axis)
    return jnp.sum(everything.astype(jnp.float32), axis=0)


def in_blocks(array, dim, count):
    before, after = (array.shape[:dim], array.shape[dim + 1 :])
    return jnp.moveaxis(array.reshape(*before, count, -1, *after), dim, 0)


def sent_and_summed(array, axis, dim):
    count = lax.axis_size(axis)
    pieces = lax.all_to_all(in_blocks(array, dim, count), axis, 0, 0, tiled=True)
    return jnp.sum(pieces, axis=0)


def rms_normalize(values):
    return values * lax.rsqrt(jnp.mean(values * values, axis=-1, keepdims=True) + EPSILON)


def sinusoid(places, width):
    index = jnp.arange(width // 2).astype(jnp.float32)
    rates = jnp.exp(index * (-2.0 * math.log(10000.0) / width))
    angles = places.astype(jnp.float32)[:, None] * rates[None, :]
    return jnp.stack([jnp.sin(angles), jnp.cos(angles)], axis=-1).reshape(places.shape[0], width)


def embed_rows(token_rows, table, places):
    vocab_range = jnp.arange(table.shape[0], dtype=jnp.int32)
    one_hot = (token_rows[:, None] == vocab_range[None, :]).astype(jnp.bfloat16)
    looked = jnp.dot(one_hot, table, preferred_element_type=jnp.float32)
    return rms_normalize(looked + sinusoid(places, table.shape[1])).astype(jnp.bfloat16)


def block_attention(queries, keys, values, blocked, head_size):
    scale = 1.0 / math.sqrt(head_size)
    head_count = queries.shape[1] // head_size
    query_rows = queries.shape[0]
    key_rows = keys.shape[0]
    query_heads = jnp.transpose(queries.reshape(query_rows, head_count, head_size), (1, 0, 2))
    key_heads = jnp.transpose(keys.reshape(key_rows, head_count, head_size), (1, 0, 2))
    value_heads = jnp.transpose(values.reshape(key_rows, head_count, head_size), (1, 0, 2))

    def one_head(operands):
        query, key, value = operands
        scores = (
            lax.dot_general(
                query, key, (((1,), (1,)), ((), ())), preferred_element_type=jnp.float32
            )
            * scale
        )
        scores = jnp.where(blocked, MASKED, scores)
        peak = jnp.max(scores, axis=1)
        weights = jnp.exp(scores - peak[:, None]).astype(jnp.bfloat16)
        total = jnp.sum(weights.astype(jnp.float32), axis=1)
        output = jnp.dot(weights, value, preferred_element_type=jnp.float32)
        return (peak, total, output)

    maxima, totals, outputs = lax.map(one_head, (query_heads, key_heads, value_heads))
    merged = jnp.transpose(outputs, (1, 0, 2)).reshape(query_rows, head_count * head_size)
    return (jnp.transpose(maxima), jnp.transpose(totals), merged)


def per_device(
    token_ids,
    latent_offset,
    embed_table,
    cross_q,
    cross_kv,
    cross_out,
    self_qkv,
    self_out,
    mlp_in,
    mlp_out,
):
    context_count = lax.axis_size("ctx")
    group_count = lax.axis_size("lat")
    context_index = lax.axis_index("ctx")
    group_index = lax.axis_index("lat")
    block_length = token_ids.shape[0]
    head_size = HD
    local_width = cross_q.shape[1]
    local_heads = local_width // head_size
    width = embed_table.shape[1]
    offset = latent_offset[0]
    latent_count = LATENTS
    row_count = latent_count // context_count
    group_rows = latent_count // group_count
    places = context_index * block_length + jnp.arange(block_length, dtype=jnp.int32)
    context = embed_rows(token_ids, embed_table, places)
    piece = lax.all_gather(cross_kv, "ctx", axis=1, tiled=True)
    columns = context
    key_sum = jnp.dot(columns, piece[0], preferred_element_type=jnp.float32)
    value_sum = jnp.dot(columns, piece[1], preferred_element_type=jnp.float32)
    keys = key_sum.astype(jnp.bfloat16)
    values = value_sum.astype(jnp.bfloat16)
    every_token = gathered_copies(token_ids, "ctx", 0)
    latent_tokens = lax.dynamic_slice_in_dim(every_token, offset, latent_count, 0)
    latent_places = offset + jnp.arange(latent_count, dtype=jnp.int32)
    latent = embed_rows(latent_tokens, embed_table, latent_places)
    columns = latent
    query_sum = jnp.dot(
        columns, gathered_copies(cross_q, "ctx", 0), preferred_element_type=jnp.float32
    )
    queries = query_sum.astype(jnp.bfloat16)
    blocked = places[None, :] > latent_places[:, None]
    maxima, totals, outputs = block_attention(queries, keys, values, blocked, head_size)
    row_start = context_index * row_count
    came_max, came_total, came_out = side_by_side(
        (maxima[:, None, :], totals[:, None, :], outputs[:, None, :]), "ctx", 0, 1, 2
    )
    peak = jnp.max(came_max, axis=1, keepdims=True)
    factor = jnp.exp(came_max - peak)
    own_totals = jnp.sum(came_total * factor, axis=1)
    spread = (
        came_out.reshape(row_count, context_count, local_heads, head_size) * factor[:, :, :, None]
    )
    own_outputs = jnp.sum(spread, axis=1).reshape(row_count, local_width)
    attended = (own_outputs / jnp.repeat(own_totals, head_size, axis=1)).astype(jnp.bfloat16)
    own_latent = lax.dynamic_slice_in_dim(latent, row_start, row_count, 0).astype(jnp.float32)
    first_stream = own_latent + of_everyone(
        jnp.dot(attended, cross_out, preferred_element_type=jnp.float32), "lat"
    )
    self_normed = rms_normalize(first_stream).astype(jnp.bfloat16)
    self_queries = jnp.dot(self_normed, self_qkv[0], preferred_element_type=jnp.float32).astype(
        jnp.bfloat16
    )
    self_keys = jnp.dot(self_normed, self_qkv[1], preferred_element_type=jnp.float32).astype(
        jnp.bfloat16
    )
    self_values = jnp.dot(self_normed, self_qkv[2], preferred_element_type=jnp.float32).astype(
        jnp.bfloat16
    )
    all_keys, all_values = side_by_side_2((self_keys, self_values), "ctx", 0, 1)
    own_places = row_start + jnp.arange(row_count, dtype=jnp.int32)
    later = jnp.arange(latent_count, dtype=jnp.int32)[None, :] > own_places[:, None]
    self_peak, self_totals, self_outputs = block_attention(
        self_queries, all_keys, all_values, later, head_size
    )
    self_attended = (self_outputs / jnp.repeat(self_totals, head_size, axis=1)).astype(jnp.bfloat16)
    second_stream = first_stream + over_copies(
        jnp.dot(self_attended, self_out, preferred_element_type=jnp.float32).astype(jnp.bfloat16),
        "lat",
    ).astype(jnp.float32)
    mlp_normed = rms_normalize(second_stream).astype(jnp.bfloat16)
    gathered = lax.all_gather(mlp_normed, "ctx", axis=0, tiled=True)
    group_input = lax.dynamic_slice_in_dim(gathered, group_index * group_rows, group_rows, 0)
    pre_hidden = jnp.dot(group_input, mlp_in, preferred_element_type=jnp.float32)
    hidden = jax.nn.gelu(pre_hidden, approximate=True).astype(jnp.bfloat16)
    place = context_index * row_count - group_index * group_rows
    inside = jnp.logical_and(place >= 0, place < group_rows)
    residual = jnp.zeros((group_rows, width), jnp.float32)
    residual = lax.dynamic_update_slice_in_dim(
        residual, second_stream, jnp.clip(place, 0, group_rows - row_count), 0
    )
    residual = jnp.where(inside, residual, 0.0)
    result = sent_and_summed(
        jnp.dot(hidden, mlp_out, preferred_element_type=jnp.float32) + residual, "ctx", 0
    )
    return result.astype(jnp.bfloat16)[None]


def solution(mesh):
    placed = (
        P("ctx"),
        P(),
        P(),
        P("ctx", "lat"),
        P(None, "ctx", "lat"),
        P("lat", None),
        P(None, None, "lat"),
        P("lat", None),
        P(None, "ctx"),
        P("ctx", None),
    )
    return jax.shard_map(
        per_device, mesh=mesh, in_specs=placed, out_specs=P("lat", "ctx", None), check_vma=False
    )
```

profile of v0, /device:TPU:1, one launch (start us, length us, event | category | flops | bytes accessed | tf_op | source)
XLA Modules:
  0.0 527.8 jit_solution(14020587515841500525)
XLA Ops:
  8.0 23.1 %all_to_all.44 = s32[64,1,512]{2,1,0:T(1,128)S(1)} all-to-all(s32[64,1,512]{2,1,0:T(1,128)S(1)} %broadcast_in_dim.52), channel_id=1, replica_groups=mesh['ctx'=64,'lat'=4] {'ctx'}, dimensions={0} | all-to-all | bytes 262144 | tf_op jit(solution)/shard_map/all_to_all | solution.py:15
  31.2 2.4 broadcast_in_dim.54
  33.6 5.8 %all-to-all-start.1 = ((bf16[64,32,512]{2,1,0:T(8,128)(2,1)}), bf16[64,32,512]{2,1,0:T(8,128)(2,1)}, u32[]{:S(2)}, u32[]{:S(2)}) async-start(bf16[64,32,512]{2,1,0:T(8,128)(2,1)} %broadcast_in_dim.54), calls=%async_computation.1 | async-start | bytes 4194304 | tf_op jit(solution)/shard_map/all_to_all | solution.py:15
  40.1 14.9 %multiply_sine_fusion = (f32[1024,1024,1]{1,0,2:T(8,128)S(1)}, f32[1024,1024,1]{1,0,2:T(8,128)S(1)}) fusion(f32[1024]{0:T(1024)S(1)} %multiply_exponential_fusion, f32[1024]{0:T(1024)S(1)} %get-tuple-element.184), kind=kLoop, calls=%fused_computation.36 | loop fusion | flops 1048576 | bytes 8396800 | tf_op jit(solution)/shard_map/sin | solution.py:83
  55.0 4.1 pad_maximum_fusion
  59.0 13.6 %copy.62 = f32[1024,1024,2]{0,2,1:T(2,128)} copy(f32[1024,1024,2]{1,0,2:T(8,128)} %pad_maximum_fusion) | data formatting | bytes 16777216 | tf_op jit(solution)/shard_map/stack | solution.py:83
  72.6 10.9 %reshape.308 = f32[1024,2048]{0,1:T(8,128)} reshape(f32[1024,1024,2]{0,2,1:T(2,128)} %copy.62) | data formatting | bytes 16777216 | tf_op jit(solution)/shard_map/reshape | solution.py:83
  83.5 9.7 %copy.63 = f32[1024,2048]{1,0:T(8,128)} copy(f32[1024,2048]{0,1:T(8,128)} %reshape.308) | data formatting | bytes 16777216 | tf_op jit(solution)/shard_map/reshape | solution.py:83
  93.2 7.3 %multiply_sine_fusion.1 = (f32[512,1024,1]{1,0,2:T(8,128)S(1)}, f32[512,1024,1]{1,0,2:T(8,128)S(1)}) fusion(f32[1024]{0:T(1024)S(1)} %multiply_exponential_fusion, f32[512]{0:T(512)S(1)} %get-tuple-element.186), kind=kLoop, calls=%fused_computation.43 | loop fusion | flops 524288 | bytes 4200448 | tf_op jit(solution)/shard_map/sin | solution.py:83
  100.6 2.3 pad_maximum_fusion.1
  102.8 7.3 %copy.65 = f32[512,1024,2]{0,2,1:T(2,128)} copy(f32[512,1024,2]{1,0,2:T(8,128)} %pad_maximum_fusion.1) | data formatting | bytes 8388608 | tf_op jit(solution)/shard_map/stack | solution.py:83
  110.1 6.1 %reshape.311 = f32[512,2048]{0,1:T(8,128)} reshape(f32[512,1024,2]{0,2,1:T(2,128)} %copy.65) | data formatting | bytes 8388608 | tf_op jit(solution)/shard_map/reshape | solution.py:83
  116.2 5.5 %copy.66 = f32[512,2048]{1,0:T(8,128)} copy(f32[512,2048]{0,1:T(8,128)} %reshape.311) | data formatting | bytes 8388608 | tf_op jit(solution)/shard_map/reshape | solution.py:83
  121.7 4.9 multiply_reduce_fusion.1
  126.7 4.6 multiply_reduce_fusion
  131.3 2.4 multiply_convert_fusion
  133.7 5.2 convolution_convert_fusion.1
  139.0 1.3 copy.64
  140.3 4.2 fusion.38
  144.8 5.1 fusion.37
  151.2 13.3 %while.28 = (s32[]{:T(128)}, f32[4,1024]{1,0:T(4,128)S(1)}, f32[4,1024]{1,0:T(4,128)S(1)}, f32[4,1024,128]{1,2,0:T(8,128)}, bf16[4,1024,128]{2,1,0:T(8,128)(2,1)...) while((s32[]{:T(128)}, f32[4,1024]{1,0:T(4,128)S(1)}, ...), condition=%wide.region_5.6_spmd.clone, body=%wide.region_2.5_spmd.clone.sunk | while | flops 274200576 | bytes 7383157 | solution.py:117
  151.2 1.4 fusion.116
  154.5 1.4 fusion.116
  157.9 1.4 fusion.116
  161.2 1.4 fusion.116
  164.6 3.3 pad_maximum_fusion.2
  167.8 6.3 %copy.70 = f32[1024,1,520]{2,1,0:T(1,128)} copy(f32[1024,1,520]{0,2,1:T(8,128)} %pad_maximum_fusion.2) | data formatting | bytes 4259840 | tf_op jit(solution)/shard_map/concatenate | solution.py:36
  174.1 72.6 %all_to_all.45 = f32[1024,1,520]{2,1,0:T(1,128)S(1)} all-to-all(f32[1024,1,520]{2,1,0:T(1,128)} %copy.70), channel_id=1, replica_groups=mesh['ctx'=64,'lat'=4] {'ctx'}, dimensions={0} | all-to-all | bytes 4259840 | tf_op jit(solution)/shard_map/all_to_all | solution.py:39
  246.9 1.4 copy-done.1
  248.6 2.2 mul.169
  250.8 3.1 mul.170
  254.0 3.0 fusion.25
  258.3 4.3 all-to-all-start.3
  262.6 9.2 %all-to-all-done.3 = f32[4,16,2048]{2,1,0:T(8,128)S(1)} async-done(((f32[4,16,2048]{2,1,0:T(8,128)}), f32[4,16,2048]{2,1,0:T(8,128)S(1)}, u32[]{:S(2)}, u32[]{:S(2)}) %all-to-all-start.3) | async-done | bytes 524320 | tf_op jit(solution)/shard_map/all_to_all | solution.py:15
  273.7 2.0 fusion.42
  275.7 2.0 fusion.45
  278.6 2.0 fusion.48
  280.6 71.2 %all-gather.6.cloned.1.call-done = bf16[1024,1024]{1,0:T(8,128)(2,1)} async-done(((bf16[16,1024]{1,0:T(8,128)(2,1)}), bf16[1024,1024]{1,0:T(8,128)(2,1)}) %all-gather.6.cloned.1.call-update) | async-done | bytes 2097168 | tf_op jit(solution)/shard_map/all_gather | solution.py:56
  351.8 1.9 slice_bitcast_fusion.8
  355.0 6.8 %while.29 = (s32[]{:T(128)}, f32[4,16]{1,0:T(4,128)S(1)}, f32[4,16,128]{2,1,0:T(8,128)S(1)}, bf16[4,16,128]{2,1,0:T(8,128)(2,1)S(1)}, bf16[4,1024,128]{2,1,0:T(8...) while((s32[]{:T(128)}, f32[4,16]{1,0:T(4,128)S(1)}, ...), condition=%wide.region_14.15_spmd.clone, body=%wide.region_11.14_spmd.clone.sunk | while | flops 8552418 | bytes 736673 | solution.py:117
  361.9 2.1 convolution_convert_fusion
  364.0 10.1 %all_to_all.46 = bf16[4,16,2048]{2,1,0:T(8,128)(2,1)S(1)} all-to-all(bf16[4,16,2048]{2,1,0:T(8,128)(2,1)S(1)} %broadcast_in_dim.106), channel_id=1, replica_groups=mesh['ctx'=64,'lat'=4] {'lat'}, dimensions={0} | all-to-all | bytes 524288 | tf_op jit(solution)/shard_map/all_to_all | solution.py:15
  375.8 76.2 %all-gather.8.cloned.1.call-done = bf16[1024,2048]{1,0:T(8,128)(2,1)} async-done(((bf16[16,2048]{1,0:T(8,128)(2,1)}), bf16[1024,2048]{1,0:T(8,128)(2,1)}) %all-gather.8.cloned.1.call-update) | async-done | bytes 4194320 | tf_op jit(solution)/shard_map/all_gather | solution.py:204
  452.0 3.5 fusion.69
  456.4 1.7 add.138
  458.1 2.9 reshape.318
  461.0 57.5 %all_to_all.47 = f32[64,4,2048]{2,1,0:T(4,128)} all-to-all(f32[64,4,2048]{2,1,0:T(4,128)} %reshape.318), channel_id=1, replica_groups=mesh['ctx'=64,'lat'=4] {'ctx'}, dimensions={0} | all-to-all | bytes 4194304 | tf_op jit(solution)/shard_map/all_to_all | solution.py:71
  518.5 2.5 reduce_sum.107
  (84 shorter events, 26.2 us)
Async XLA Ops:
  6.5 250.5 %copy-start = (bf16[512,2048]{1,0:T(8,128)(2,1)S(1)}, bf16[512,2048]{1,0:T(8,128)(2,1)}, u32[]{:S(2)}) copy-start(bf16[512,2048]{1,0:T(8,128)(2,1)} %param.19) | copy-start | bytes 6291460
  6.5 133.8 %all-gather.4.cloned.1.call-start = ((), (), s32[]{:S(2)}) async-start(), calls=%async_computation.6 | async-start | bytes 4259840 | tf_op jit(solution)/shard_map/all_gather | solution.py:149
  33.6 100.2 %all-to-all-start.1 = ((bf16[64,32,512]{2,1,0:T(8,128)(2,1)}), bf16[64,32,512]{2,1,0:T(8,128)(2,1)}, u32[]{:S(2)}, u32[]{:S(2)}) async-start(bf16[64,32,512]{2,1,0:T(8,128)(2,1)} %broadcast_in_dim.54), calls=%async_computation.1 | async-start | bytes 4194304 | tf_op jit(solution)/shard_map/all_to_all | solution.py:15
  116.2 5.5 %copy-start.2 = (bf16[256,2048]{1,0:T(8,128)(2,1)S(1)}, bf16[256,2048]{1,0:T(8,128)(2,1)}, u32[]{:S(2)}) copy-start(bf16[256,2048]{1,0:T(8,128)(2,1)} %param.16) | copy-start | bytes 3145732
  116.2 5.5 %copy-start.4 = (s32[512]{0:T(512)S(1)}, s32[512]{0:T(512)}, u32[]{:S(2)}) copy-start(s32[512]{0:T(512)} %param.14) | copy-start | bytes 6148
  246.8 1.5 copy-start.1
  258.3 13.5 %all-to-all-start.3 = ((f32[4,16,2048]{2,1,0:T(8,128)}), f32[4,16,2048]{2,1,0:T(8,128)S(1)}, u32[]{:S(2)}, u32[]{:S(2)}) async-start(f32[4,16,2048]{2,1,0:T(8,128)} %broadcast_in_dim.58), calls=%async_computation.3 | async-start | bytes 1048576 | tf_op jit(solution)/shard_map/all_to_all | solution.py:15
  262.6 89.2 %all-gather.6.cloned.1.call-start = ((), (), s32[]{:S(2)}) async-start(), calls=%async_computation.7 | async-start | bytes 2129920 | tf_op jit(solution)/shard_map/all_gather | solution.py:56
  278.3 173.7 %all-gather.8.cloned.1.call-start = ((), (), s32[]{:S(2)}) async-start(), calls=%async_computation.8 | async-start | bytes 4259840 | tf_op jit(solution)/shard_map/all_gather | solution.py:204
  361.9 90.2 %copy-start.3 = (bf16[128,2048]{1,0:T(8,128)(2,1)S(1)}, bf16[128,2048]{1,0:T(8,128)(2,1)}, u32[]{:S(2)}) copy-start(bf16[128,2048]{1,0:T(8,128)(2,1)} %param.23) | copy-start | bytes 1572868
Sparse Core Ops, SparseCore 0:
  10.2 92.9 all-gather.3
  278.4 73.3 all-gather.5
  375.9 76.0 all-gather.7
where the time goes:
time: 533 us; the launch traced here: 528 us
  blocking collectives  163 us (31%)
  waiting for transfers between devices  157 us (29%)
  local copies, waits for them, and re-layouts  81.8 us (15%)
  matrix products  52.1 us (10%)
  other arithmetic  48.5 us (9%)
  between operations  14.2 us (3%)
  starting transfers between devices  10.4 us (2%)
    all_gather x1, waiting for transfers between devices, per_device(): gathered = lax.all_gather(mlp_normed, 'ctx', axis=0, tiled=True)  76.2 us
    all_to_all x1, blocking collectives, side_by_side(): lax.all_to_all(both, axis, split_axis=split_dim, concat_axis=concat_dim,...  72.6 us
    all_gather x1, waiting for transfers between devices, side_by_side_2(): lax.all_gather(both, axis, axis=dim, tiled=True)  71.2 us
    all_to_all x1, blocking collectives, sent_and_summed(): lax.all_to_all(in_blocks(array, dim, count), axis, 0, 0, tiled=True)  57.5 us
    all_to_all x2, blocking collectives, sent_to_all(): lax.all_to_all(jnp.broadcast_to(array[None], (count, *array.shape)), axis...  33.2 us
    reshape x4, local copies, waits for them, and re-layouts, sinusoid(): jnp.stack([jnp.sin(angles), jnp.cos(angles)], axis=-1)  32.2 us
    sin x2, other arithmetic, sinusoid(): jnp.sin(angles)  22.2 us
    another operation x2, local copies, waits for them, and re-layouts, sinusoid(): jnp.stack([jnp.sin(angles), jnp.cos(angles)], axis=-1)  20.8 us
  transfers between devices with their start and end apart: 5, of which 3 were waited for; matrix products, arithmetic and copies ran while one was open for 20% of the time, Pallas kernels for 0%

commit v1 on v0

--- a/solution.py
+++ b/solution.py
@@ -8,6 +8,12 @@
 LATENTS = 1024
 EPSILON = 1e-06
 MASKED = -1e30
+
+
+def gather_from_all(x, axis, dim):
+    size = lax.axis_size(axis)
+    repeats = [size if d == dim else 1 for d in range(x.ndim)]
+    return lax.all_to_all(jnp.tile(x, repeats), axis, split_axis=dim, concat_axis=dim, tiled=True)
 
 
 def sent_to_all(array, axis):
@@ -201,7 +207,7 @@
         "lat",
     ).astype(jnp.float32)
     mlp_normed = rms_normalize(second_stream).astype(jnp.bfloat16)
-    gathered = lax.all_gather(mlp_normed, "ctx", axis=0, tiled=True)
+    gathered = gather_from_all(mlp_normed, "ctx", 0)
     group_input = lax.dynamic_slice_in_dim(gathered, group_index * group_rows, group_rows, 0)
     pre_hidden = jnp.dot(group_input, mlp_in, preferred_element_type=jnp.float32)
     hidden = jax.nn.gelu(pre_hidden, approximate=True).astype(jnp.bfloat16)

time: 533 us -> 562 us (1.054)
  waiting for transfers between devices: 157 us -> 177 us
  starting transfers between devices: 10.4 us -> 18.5 us
    all_to_all x0 -> x1, waiting for transfers between devices: none -> 95.9 us  [gather_from_all(): lax.all_to_all(jnp.tile(x, repeats), axis, split_axis=dim, concat_axis=di...]
    all_gather x1 -> x0, waiting for transfers between devices: 76.2 us -> none  [per_device(): gathered = lax.all_gather(mlp_normed, 'ctx', axis=0, tiled=True)]
    all_to_all x0 -> x1, starting transfers between devices: none -> 8.13 us  [gather_from_all(): lax.all_to_all(jnp.tile(x, repeats), axis, split_axis=dim, concat_axis=di...]
  transfers between devices with their start and end apart: 5 -> 5, of which waited for: 3 -> 3; matrix products, arithmetic and copies ran while one was open for 20% -> 19% of each run, Pallas kernels for 0% -> 0%
where the time goes in v1:
time: 562 us; the launch traced here: 557 us
  waiting for transfers between devices  177 us (31%)
  blocking collectives  163 us (29%)
  local copies, waits for them, and re-layouts  84.3 us (15%)
  matrix products  51.9 us (9%)
  other arithmetic  47.8 us (9%)
  starting transfers between devices  18.5 us (3%)
  between operations  14.6 us (3%)
    all_to_all x1, waiting for transfers between devices, gather_from_all(): lax.all_to_all(jnp.tile(x, repeats), axis, split_axis=dim, concat_axis=di...  95.9 us
    all_to_all x1, blocking collectives, side_by_side(): lax.all_to_all(both, axis, split_axis=split_dim, concat_axis=concat_dim,...  72.6 us
    all_gather x1, waiting for transfers between devices, side_by_side_2(): lax.all_gather(both, axis, axis=dim, tiled=True)  71.5 us
    all_to_all x1, blocking collectives, sent_and_summed(): lax.all_to_all(in_blocks(array, dim, count), axis, 0, 0, tiled=True)  57 us
    all_to_all x2, blocking collectives, sent_to_all(): lax.all_to_all(jnp.broadcast_to(array[None], (count, *array.shape)), axis...  33.2 us
    reshape x4, local copies, waits for them, and re-layouts, sinusoid(): jnp.stack([jnp.sin(angles), jnp.cos(angles)], axis=-1)  32.2 us
    sin x2, other arithmetic, sinusoid(): jnp.sin(angles)  22.2 us
    another operation x2, local copies, waits for them, and re-layouts, sinusoid(): jnp.stack([jnp.sin(angles), jnp.cos(angles)], axis=-1)  20.8 us
  transfers between devices with their start and end apart: 5, of which 3 were waited for; matrix products, arithmetic and copies ran while one was open for 19% of the time, Pallas kernels for 0%

profile of v1, /device:TPU:1, one launch (start us, length us, event | category | flops | bytes accessed | tf_op | source)
XLA Modules:
  0.0 557.0 jit_solution(4517891871602698431)
XLA Ops:
  8.0 23.1 %all_to_all.53 = s32[64,1,512]{2,1,0:T(1,128)S(1)} all-to-all(s32[64,1,512]{2,1,0:T(1,128)S(1)} %broadcast_in_dim.52), channel_id=1, replica_groups=mesh['ctx'=64,'lat'=4] {'ctx'}, dimensions={0} | all-to-all | bytes 262144 | tf_op jit(solution)/shard_map/all_to_all | solution.py:21
  31.2 2.4 broadcast_in_dim.54
  33.6 5.8 %all-to-all-start.1 = ((bf16[64,32,512]{2,1,0:T(8,128)(2,1)}), bf16[64,32,512]{2,1,0:T(8,128)(2,1)}, u32[]{:S(2)}, u32[]{:S(2)}) async-start(bf16[64,32,512]{2,1,0:T(8,128)(2,1)} %broadcast_in_dim.54), calls=%async_computation.1 | async-start | bytes 4194304 | tf_op jit(solution)/shard_map/all_to_all | solution.py:21
  40.1 14.9 %multiply_sine_fusion = (f32[1024,1024,1]{1,0,2:T(8,128)S(1)}, f32[1024,1024,1]{1,0,2:T(8,128)S(1)}) fusion(f32[1024]{0:T(1024)S(1)} %multiply_exponential_fusion, f32[1024]{0:T(1024)S(1)} %get-tuple-element.184), kind=kLoop, calls=%fused_computation.36 | loop fusion | flops 1048576 | bytes 8396800 | tf_op jit(solution)/shard_map/sin | solution.py:89
  55.0 4.1 pad_maximum_fusion
  59.0 13.6 %copy.62 = f32[1024,1024,2]{0,2,1:T(2,128)} copy(f32[1024,1024,2]{1,0,2:T(8,128)} %pad_maximum_fusion) | data formatting | bytes 16777216 | tf_op jit(solution)/shard_map/stack | solution.py:89
  72.6 10.9 %reshape.315 = f32[1024,2048]{0,1:T(8,128)} reshape(f32[1024,1024,2]{0,2,1:T(2,128)} %copy.62) | data formatting | bytes 16777216 | tf_op jit(solution)/shard_map/reshape | solution.py:89
  83.5 9.7 %copy.63 = f32[1024,2048]{1,0:T(8,128)} copy(f32[1024,2048]{0,1:T(8,128)} %reshape.315) | data formatting | bytes 16777216 | tf_op jit(solution)/shard_map/reshape | solution.py:89
  93.2 7.3 %multiply_sine_fusion.1 = (f32[512,1024,1]{1,0,2:T(8,128)S(1)}, f32[512,1024,1]{1,0,2:T(8,128)S(1)}) fusion(f32[1024]{0:T(1024)S(1)} %multiply_exponential_fusion, f32[512]{0:T(512)S(1)} %get-tuple-element.186), kind=kLoop, calls=%fused_computation.43 | loop fusion | flops 524288 | bytes 4200448 | tf_op jit(solution)/shard_map/sin | solution.py:89
  100.6 2.3 pad_maximum_fusion.1
  102.8 7.3 %copy.65 = f32[512,1024,2]{0,2,1:T(2,128)} copy(f32[512,1024,2]{1,0,2:T(8,128)} %pad_maximum_fusion.1) | data formatting | bytes 8388608 | tf_op jit(solution)/shard_map/stack | solution.py:89
  110.1 6.1 %reshape.318 = f32[512,2048]{0,1:T(8,128)} reshape(f32[512,1024,2]{0,2,1:T(2,128)} %copy.65) | data formatting | bytes 8388608 | tf_op jit(solution)/shard_map/reshape | solution.py:89
  116.2 5.5 copy.66
  121.7 4.9 multiply_reduce_fusion.1
  126.7 4.6 multiply_reduce_fusion
  131.3 2.4 multiply_convert_fusion
  133.7 5.2 convolution_convert_fusion.1
  140.3 4.2 fusion.38
  144.8 5.1 fusion.37
  151.2 13.3 %while.28 = (s32[]{:T(128)}, f32[4,1024]{1,0:T(4,128)S(1)}, f32[4,1024]{1,0:T(4,128)S(1)}, f32[4,1024,128]{1,2,0:T(8,128)}, bf16[4,1024,128]{2,1,0:T(8,128)(2,1)...) while((s32[]{:T(128)}, f32[4,1024]{1,0:T(4,128)S(1)}, ...), condition=%wide.region_5.6_spmd.clone, body=%wide.region_2.5_spmd.clone.sunk | while | flops 274200576 | bytes 7383157 | solution.py:123
  151.2 1.4 fusion.116
  154.5 1.4 fusion.116
  157.9 1.4 fusion.116
  164.6 3.3 pad_maximum_fusion.2
  167.8 6.3 %copy.70 = f32[1024,1,520]{2,1,0:T(1,128)} copy(f32[1024,1,520]{0,2,1:T(8,128)} %pad_maximum_fusion.2) | data formatting | bytes 4259840 | tf_op jit(solution)/shard_map/concatenate | solution.py:42
  174.1 72.6 %all_to_all.54 = f32[1024,1,520]{2,1,0:T(1,128)S(1)} all-to-all(f32[1024,1,520]{2,1,0:T(1,128)} %copy.70), channel_id=1, replica_groups=mesh['ctx'=64,'lat'=4] {'ctx'}, dimensions={0} | all-to-all | bytes 4259840 | tf_op jit(solution)/shard_map/all_to_all | solution.py:45
  246.9 1.4 copy-done.1
  248.6 2.2 mul.169
  250.8 3.1 mul.170
  254.0 3.0 fusion.25
  258.3 4.3 all-to-all-start.3
  262.8 8.9 %all-to-all-done.3 = f32[4,16,2048]{2,1,0:T(8,128)S(1)} async-done(((f32[4,16,2048]{2,1,0:T(8,128)}), f32[4,16,2048]{2,1,0:T(8,128)S(1)}, u32[]{:S(2)}, u32[]{:S(2)}) %all-to-all-start.3) | async-done | bytes 524320 | tf_op jit(solution)/shard_map/all_to_all | solution.py:21
  273.7 2.0 fusion.42
  275.7 2.0 fusion.45
  278.3 2.0 fusion.48
  280.3 71.5 %all-gather.5.cloned.1.call-done = bf16[1024,1024]{1,0:T(8,128)(2,1)} async-done(((bf16[16,1024]{1,0:T(8,128)(2,1)}), bf16[1024,1024]{1,0:T(8,128)(2,1)}) %all-gather.5.cloned.1.call-update) | async-done | bytes 2097168 | tf_op jit(solution)/shard_map/all_gather | solution.py:62
  351.8 1.9 slice_bitcast_fusion.8
  355.0 6.8 %while.29 = (s32[]{:T(128)}, f32[4,16]{1,0:T(4,128)S(1)}, f32[4,16,128]{2,1,0:T(8,128)S(1)}, bf16[4,16,128]{2,1,0:T(8,128)(2,1)S(1)}, bf16[4,1024,128]{2,1,0:T(8...) while((s32[]{:T(128)}, f32[4,16]{1,0:T(4,128)S(1)}, ...), condition=%wide.region_14.15_spmd.clone, body=%wide.region_11.14_spmd.clone.sunk | while | flops 8552418 | bytes 736673 | solution.py:123
  361.9 2.0 convolution_convert_fusion
  363.9 10.1 %all_to_all.55 = bf16[4,16,2048]{2,1,0:T(8,128)(2,1)S(1)} all-to-all(bf16[4,16,2048]{2,1,0:T(8,128)(2,1)S(1)} %broadcast_in_dim.106), channel_id=1, replica_groups=mesh['ctx'=64,'lat'=4] {'lat'}, dimensions={0} | all-to-all | bytes 524288 | tf_op jit(solution)/shard_map/all_to_all | solution.py:21
  375.1 2.5 tile.2
  377.6 8.1 %all-to-all-start.5 = ((bf16[64,16,2048]{2,1,0:T(8,128)(2,1)}), bf16[64,16,2048]{2,1,0:T(8,128)(2,1)}, u32[]{:S(2)}, u32[]{:S(2)}) async-start(bf16[64,16,2048]{2,1,0:T(8,128)(2,1)} %tile.2), calls=%async_computation.5 | async-start | bytes 8388608 | tf_op jit(solution)/shard_map/all_to_all | solution.py:16
  385.7 95.9 %all-to-all-done.5 = bf16[64,16,2048]{2,1,0:T(8,128)(2,1)} async-done(((bf16[64,16,2048]{2,1,0:T(8,128)(2,1)}), bf16[64,16,2048]{2,1,0:T(8,128)(2,1)}, u32[]{:S(2)}, u32[]{:S(2)}) %all-to-all-start.5) | async-done | bytes 4194336 | tf_op jit(solution)/shard_map/all_to_all | solution.py:16
  481.6 3.3 fusion.69
  485.9 1.7 add.138
  487.6 2.9 reshape.325
  490.5 57.0 %all_to_all.56 = f32[64,4,2048]{2,1,0:T(4,128)} all-to-all(f32[64,4,2048]{2,1,0:T(4,128)} %reshape.325), channel_id=1, replica_groups=mesh['ctx'=64,'lat'=4] {'ctx'}, dimensions={0} | all-to-all | bytes 4194304 | tf_op jit(solution)/shard_map/all_to_all | solution.py:77
  547.5 2.5 reduce_sum.107
  (86 shorter events, 28.2 us)
Async XLA Ops:
  6.5 250.5 %copy-start = (bf16[512,2048]{1,0:T(8,128)(2,1)S(1)}, bf16[512,2048]{1,0:T(8,128)(2,1)}, u32[]{:S(2)}) copy-start(bf16[512,2048]{1,0:T(8,128)(2,1)} %param.19) | copy-start | bytes 6291460
  6.5 133.8 %all-gather.3.cloned.1.call-start = ((), (), s32[]{:S(2)}) async-start(), calls=%async_computation.7 | async-start | bytes 4259840 | tf_op jit(solution)/shard_map/all_gather | solution.py:155
  33.6 100.2 %all-to-all-start.1 = ((bf16[64,32,512]{2,1,0:T(8,128)(2,1)}), bf16[64,32,512]{2,1,0:T(8,128)(2,1)}, u32[]{:S(2)}, u32[]{:S(2)}) async-start(bf16[64,32,512]{2,1,0:T(8,128)(2,1)} %broadcast_in_dim.54), calls=%async_computation.1 | async-start | bytes 4194304 | tf_op jit(solution)/shard_map/all_to_all | solution.py:21
  116.2 5.5 copy-start.2
  116.2 5.5 copy-start.5
  246.8 1.5 copy-start.1
  258.3 13.5 %all-to-all-start.3 = ((f32[4,16,2048]{2,1,0:T(8,128)}), f32[4,16,2048]{2,1,0:T(8,128)S(1)}, u32[]{:S(2)}, u32[]{:S(2)}) async-start(f32[4,16,2048]{2,1,0:T(8,128)} %broadcast_in_dim.58), calls=%async_computation.3 | async-start | bytes 1048576 | tf_op jit(solution)/shard_map/all_to_all | solution.py:21
  262.6 89.2 %all-gather.5.cloned.1.call-start = ((), (), s32[]{:S(2)}) async-start(), calls=%async_computation.8 | async-start | bytes 2129920 | tf_op jit(solution)/shard_map/all_gather | solution.py:62
  377.6 104.0 %copy-start.3 = (bf16[128,2048]{1,0:T(8,128)(2,1)S(1)}, bf16[128,2048]{1,0:T(8,128)(2,1)}, u32[]{:S(2)}) copy-start(bf16[128,2048]{1,0:T(8,128)(2,1)} %param.23) | copy-start | bytes 1572868
  377.6 104.0 %copy-start.4 = (bf16[2048,128]{1,0:T(8,128)(2,1)S(1)}, bf16[2048,128]{1,0:T(8,128)(2,1)}, u32[]{:S(2)}) copy-start(bf16[2048,128]{1,0:T(8,128)(2,1)} %param.22) | copy-start | bytes 1572868
  377.6 104.0 %all-to-all-start.5 = ((bf16[64,16,2048]{2,1,0:T(8,128)(2,1)}), bf16[64,16,2048]{2,1,0:T(8,128)(2,1)}, u32[]{:S(2)}, u32[]{:S(2)}) async-start(bf16[64,16,2048]{2,1,0:T(8,128)(2,1)} %tile.2), calls=%async_computation.5 | async-start | bytes 8388608 | tf_op jit(solution)/shard_map/all_to_all | solution.py:16
Sparse Core Ops, SparseCore 0:
  10.2 92.9 all-gather.2
  278.4 73.3 all-gather.4
